TPU v7x, 32 devices: a whole 2x2x4 slice. The times are simulated.
32 devices in a mesh: dp: 8 (over z, x), expert: 4 (over y, core).
Axes of the slice: x: 2, y: 2, z: 4, core: 2. Of those that a mesh axis runs over, the one named last changes fastest.
Arguments:
- tokens: bfloat16 [4096, 1280], P(('dp', 'expert')), may hold values from -6 to 6
- routes: int32 [4096, 2], P(('dp', 'expert')), may hold values from 0 to 31, all different within a row; in each aligned block of 128 rows (0 to 127, 128 to 255, ...) at most 10 rows name the same one
- combine: float32 [4096, 2], P(('dp', 'expert')), may hold values from 0.1 to 1
- w_in: bfloat16 [1280, 163840], P(None, ('dp', 'expert')), may hold values from -0.15625 to 0.15625
- w_out: bfloat16 [163840, 1280], P(('dp', 'expert')), may hold values from -0.078125 to 0.078125
- out_grad: bfloat16 [4096, 1280], P(('dp', 'expert')), may hold values from -6 to 6
- head_w: bfloat16 [1280, 17408], P(None, 'expert'), may hold values from -0.5 to 0.5
- labels: int32 [16, 4], P('dp'), may hold values from 0 to 17407
Outputs:
- mixed_out: bfloat16 [4096, 1280], P(('dp', 'expert'))
- d_tokens: bfloat16 [4096, 1280], P(('dp', 'expert'))
- d_combine: float32 [4096, 2], P(('dp', 'expert'))
- d_w_in: bfloat16 [1280, 163840], P(None, ('dp', 'expert'))
- d_w_out: bfloat16 [163840, 1280], P(('dp', 'expert'))
- image_loss: float32 [16], P('dp')
- d_pooled: float32 [16, 1280], P('dp')
- d_head: bfloat16 [1280, 17408], P('dp', 'expert')
Inputs may be any that keep to these rules, and one draw needn't show every extreme that they name: `routes`: in the 128 rows of each device no expert is named by more than 10 rows, a bound that some block reaches; the two entries of a row differ. `labels`: entries of one image may repeat.
All inputs are finite; a program needn't handle non-finite values.
Results may differ from a plain program's by a relative error of at most 0.015.
Values may be sent and summed in bfloat16 or wider, within the bound.
A program may use at most 192 MiB of HBM per device.

v0:
```python
import jax
import jax.numpy as jnp
from jax import lax
from jax.sharding import PartitionSpec as P

D = 1280
EXPERTS = 32
PATCHES = 256
CLASSES = 17408


beta_rate = 0.99
norm_eps = 1e-06


def gelu_fn(values):
    return jax.nn.gelu(values, approximate=True)


def normalize(pooled):
    center = jnp.mean(pooled, axis=1, keepdims=True)
    spread = jnp.mean(jnp.square(pooled - center), axis=1, keepdims=True)
    return (pooled - center) * lax.rsqrt(spread + norm_eps)


def weighted_focal(logit_vals, targets, class_weight):
    nll_vals = targets * jax.nn.softplus(-logit_vals) + (1.0 - targets) * jax.nn.softplus(
        logit_vals
    )
    return class_weight[None, :] * jnp.square(1.0 - jnp.exp(-nll_vals)) * nll_vals


def expert_pass(xs_rows, grad_rows, w_first, w_second):
    h_pre = jnp.dot(xs_rows, w_first, preferred_element_type=jnp.float32)
    hidden, gelu_back = jax.vjp(gelu_fn, h_pre)
    hidden_bf = hidden.astype(jnp.bfloat16)
    expert_out = jnp.dot(hidden_bf, w_second, preferred_element_type=jnp.float32)
    d_hidden = lax.dot_general(
        grad_rows, w_second, (((1,), (1,)), ((), ())), preferred_element_type=jnp.float32
    )
    d_pre = gelu_back(d_hidden)[0].astype(jnp.bfloat16)
    d_second = lax.dot_general(
        hidden_bf, grad_rows, (((0,), (0,)), ((), ())), preferred_element_type=jnp.float32
    ).astype(jnp.bfloat16)
    d_first = lax.dot_general(
        xs_rows, d_pre, (((0,), (0,)), ((), ())), preferred_element_type=jnp.float32
    ).astype(jnp.bfloat16)
    d_rows = lax.dot_general(
        d_pre, w_first, (((1,), (1,)), ((), ())), preferred_element_type=jnp.float32
    )
    return (expert_out, d_rows, d_first, d_second)


def to_experts(stacked):
    return lax.all_to_all(stacked, ("dp", "expert"), split_axis=1, concat_axis=1, tiled=True)


def to_sources(partials):
    return lax.all_to_all(partials, ("dp", "expert"), split_axis=0, concat_axis=0, tiled=True)


def shards(tokens, routes, combine, w_in, w_out, out_grad, head_w, labels):
    dp_size = lax.axis_size("dp")
    ex_size = lax.axis_size("expert")
    n_devices = dp_size * ex_size
    tok_rows = tokens.shape[0]
    capacity = 5 * tok_rows // 64
    share_count = n_devices // EXPERTS
    buffer_rows = EXPERTS * capacity
    flat_routes = routes.reshape(tok_rows * 2)
    route_hits = (flat_routes[:, None] == jnp.arange(EXPERTS, dtype=jnp.int32)[None, :]).astype(
        jnp.int32
    )
    earlier = jnp.cumsum(route_hits, axis=0) - route_hits
    slot_pos = jnp.sum(earlier * route_hits, axis=1)
    slot_index = flat_routes * capacity + slot_pos
    pair_table = (jnp.arange(buffer_rows, dtype=jnp.int32)[:, None] == slot_index[None, :]).astype(
        jnp.bfloat16
    )
    token_table = jnp.sum(pair_table.reshape(buffer_rows, tok_rows, 2), axis=2)
    pair_grad = (
        (combine[:, :, None] * out_grad.astype(jnp.float32)[:, None, :])
        .astype(jnp.bfloat16)
        .reshape(tok_rows * 2, D)
    )
    x_buf = jnp.dot(token_table, tokens, preferred_element_type=jnp.float32).astype(jnp.bfloat16)
    g_buf = jnp.dot(pair_table, pair_grad, preferred_element_type=jnp.float32).astype(jnp.bfloat16)
    stacked = jnp.stack([x_buf, g_buf]).reshape(2, EXPERTS, 1, capacity, D)
    stacked = jnp.broadcast_to(stacked, (2, EXPERTS, share_count, capacity, D)).reshape(
        2, n_devices, capacity, D
    )
    arrived = to_experts(stacked)
    xs_rows = arrived[0].reshape(n_devices * capacity, D)
    grad_rows = arrived[1].reshape(n_devices * capacity, D)
    expert_out, d_rows, d_w_in, d_w_out = expert_pass(xs_rows, grad_rows, w_in, w_out)
    back_out = to_sources(expert_out.reshape(n_devices, capacity, D))
    expert_sum = jnp.sum(back_out.reshape(EXPERTS, share_count, capacity, D), axis=1).reshape(
        buffer_rows, D
    )
    expert_vals = jnp.take(expert_sum, slot_index, axis=0).reshape(tok_rows, 2, D)
    mixed_out = (
        tokens.astype(jnp.float32) + jnp.sum(combine[:, :, None] * expert_vals, axis=1)
    ).astype(jnp.bfloat16)
    d_combine = jnp.sum(out_grad.astype(jnp.float32)[:, None, :] * expert_vals, axis=2)
    ex_index = lax.axis_index("expert")
    row_images = ex_size * tok_rows // PATCHES
    token_image = (ex_index * tok_rows + jnp.arange(tok_rows, dtype=jnp.int32)) // PATCHES
    image_table = (jnp.arange(row_images, dtype=jnp.int32)[:, None] == token_image[None, :]).astype(
        jnp.float32
    )
    pooled_part = jnp.dot(
        image_table, mixed_out.astype(jnp.float32), precision=lax.Precision.HIGHEST
    )
    class_cols = head_w.shape[1]
    class_ids = ex_index * class_cols + jnp.arange(class_cols, dtype=jnp.int32)
    targets = jnp.any(labels[:, :, None] == class_ids[None, None, :], axis=1).astype(jnp.float32)
    counts = lax.psum(jnp.sum(targets, axis=0), "dp")
    effective = (1.0 - beta_rate) / (1.0 - jnp.power(beta_rate, counts + 1.0))
    pooled_sum, effective_total = lax.psum((pooled_part, jnp.sum(effective)), "expert")
    back_parts = to_sources(d_rows.reshape(n_devices, capacity, D))
    back_sum = jnp.sum(back_parts.reshape(EXPERTS, share_count, capacity, D), axis=1).reshape(
        buffer_rows, D
    )
    expert_back = jnp.take(back_sum, slot_index, axis=0).reshape(tok_rows, 2, D)
    d_tokens = (out_grad.astype(jnp.float32) + jnp.sum(expert_back, axis=1)).astype(jnp.bfloat16)
    class_weight = effective * CLASSES / effective_total
    pooled = pooled_sum / PATCHES
    normed, norm_back = jax.vjp(normalize, pooled)
    normed_bf = normed.astype(jnp.bfloat16)
    logits = jnp.dot(normed_bf, head_w, preferred_element_type=jnp.float32)
    focal_terms, focal_back = jax.vjp(
        lambda logit_vals: weighted_focal(logit_vals, targets, class_weight), logits
    )
    d_logits = focal_back(jnp.ones_like(focal_terms))[0].astype(jnp.bfloat16)
    normed_part = lax.dot_general(
        d_logits, head_w, (((1,), (1,)), ((), ())), preferred_element_type=jnp.float32
    )
    d_normed, image_loss = lax.psum((normed_part, jnp.sum(focal_terms, axis=1)), "expert")
    d_pooled = norm_back(d_normed)[0]
    d_head = lax.psum_scatter(
        lax.dot_general(
            normed_bf, d_logits, (((0,), (0,)), ((), ())), preferred_element_type=jnp.float32
        ).astype(jnp.bfloat16),
        "dp",
        scatter_dimension=0,
        tiled=True,
    )
    return (mixed_out, d_tokens, d_combine, d_w_in, d_w_out, image_loss, d_pooled, d_head)


def solution(mesh):
    in_specs = (
        P(("dp", "expert"), None),
        P(("dp", "expert"), None),
        P(("dp", "expert"), None),
        P(None, ("dp", "expert")),
        P(("dp", "expert"), None),
        P(("dp", "expert"), None),
        P(None, "expert"),
        P("dp", None),
    )
    out_specs = (
        P(("dp", "expert"), None),
        P(("dp", "expert"), None),
        P(("dp", "expert"), None),
        P(None, ("dp", "expert")),
        P(("dp", "expert"), None),
        P("dp"),
        P("dp", None),
        P("dp", "expert"),
    )
    return jax.shard_map(shards, mesh=mesh, in_specs=in_specs, out_specs=out_specs, check_vma=False)
```

profile of v0, /device:TPU:0, one launch (start us, length us, event | category | flops | bytes accessed | tf_op | source)
XLA Modules:
  0.0 502.4 jit_solution(1925474301695870536)
XLA Ops:
  7.2 0.8 copy.46
  9.3 0.8 reduce_sum.141
  10.0 1.3 mul.203
  11.3 0.9 mul.204
  12.3 0.8 copy.45
  14.0 0.9 copy.49
  15.0 1.3 convolution_convert_fusion.4
  16.3 1.2 stack.9
  17.5 1.6 pad_maximum_fusion
  19.2 1.7 copy.51
  20.8 46.5 %all_to_all.15 = bf16[2,32,10,1280]{3,0,2,1:T(2,128)(2,1)S(1)} all-to-all(bf16[2,32,10,1280]{3,0,2,1:T(2,128)(2,1)S(1)} %copy.51), channel_id=1, replica_groups=mesh['dp'=8,'expert'=4] {'dp','expert'}, dimensions={1} | all-to-all | bytes 3276800 | tf_op jit(solution)/shard_map/all_to_all | solution.py:55
  67.3 8.4 %slice_reduce_fusion = (bf16[32,10,1280]{2,1,0:T(8,128)(2,1)}, bf16[32,10,1280]{2,1,0:T(8,128)(2,1)}) fusion(bf16[2,32,10,1280]{3,0,2,1:T(2,128)(2,1)S(1)} %all_to_all.15), kind=kLoop, calls=%fused_computation.18 | loop fusion | bytes 3276800 | tf_op jit(solution)/shard_map/slice | solution.py:94
  75.7 1.4 reshape_squeeze.7
  77.2 1.7 reshape_squeeze.6
  78.9 15.5 %fusion.38 = f32[320,5120]{1,0:T(8,128)} fusion(bf16[320,1280]{1,0:T(8,128)(2,1)S(1)} %reshape_squeeze.7, bf16[5120,1280]{1,0:T(8,128)(2,1)} %param.15), kind=kOutput, calls=%fused_computation.99 | convolution fusion | flops 4194304000 | bytes 20480000 | tf_op jit(solution)/shard_map/dot_general | solution.py:38
  94.5 13.4 %fusion.6 = (bf16[320,5120]{1,0:T(8,128)(2,1)S(1)}, f32[320,5120]{1,0:T(8,128)}) fusion(f32[320,5120]{1,0:T(8,128)} %fusion.38, bf16[320,1280]{1,0:T(8,128)(2,1)S(1)} %reshape_squeeze.6, bf16[1280,5120]{1,0:T(8,128)(2,1)} %param.14), kind=kOutput, calls=%fused_computation.13 | convolution fusion | flops 4227072000 | bytes 30310400 | tf_op jit(solution)/shard_map/dot_general | solution.py:34
  107.9 1.7 copy-done.9
  109.6 7.5 %fusion.39 = f32[320,1280]{1,0:T(8,128)S(1)} fusion(bf16[320,5120]{1,0:T(8,128)(2,1)S(1)} %get-tuple-element.64, bf16[1280,5120]{1,0:T(8,128)(2,1)} %param.14), kind=kOutput, calls=%fused_computation.100 | convolution fusion | flops 4194304000 | bytes 18022400 | tf_op jit(solution)/shard_map/dot_general | solution.py:48
  117.1 1.6 reshape.150
  118.8 3.5 all-to-all-start.2
  122.3 11.5 %fusion.37 = f32[320,1280]{1,0:T(8,128)S(1)} fusion(bf16[5120,1280]{1,0:T(8,128)(2,1)} %param.15, f32[320,5120]{1,0:T(8,128)} %get-tuple-element.65), kind=kOutput, calls=%fused_computation.98 | convolution fusion | flops 4209049600 | bytes 21299200 | tf_op jit(solution)/shard_map/dot_general | solution.py:37
  133.8 1.6 reshape.147
  135.4 47.1 %all-to-all-done.2 = f32[32,10,1280]{2,1,0:T(8,128)} async-done(((f32[32,10,1280]{2,1,0:T(8,128)}), f32[32,10,1280]{2,1,0:T(8,128)}, u32[]{:S(2)}, u32[]{:S(2)}) %all-to-all-start.2) | async-done | bytes 1638432 | tf_op jit(solution)/shard_map/all_to_all | solution.py:59
  182.6 4.4 all-to-all-start.1
  187.2 83.0 %psum.35 = f32[4352]{0:T(1024)S(1)} all-reduce(f32[4352]{0:T(1024)S(1)} %convert_reduce_fusion), channel_id=1, replica_groups=mesh['dp'=8,'expert'=4] {'dp'}, use_global_device_ids=true, to_apply=%region_9.11 | all-reduce | flops 4352 | bytes 34816 | tf_op jit(solution)/shard_map/psum | solution.py:117
  270.3 0.6 fusion.27
  270.9 1.8 reshape.151
  272.8 2.3 gather_fusion.1
  275.0 1.8 reshape.148
  276.9 2.2 gather_fusion
  279.1 3.1 multiply_reduce_fusion
  282.2 2.1 reshape.149
  284.3 1.6 multiply_reduce_fusion.1
  286.2 11.5 %all-reduce.1 = (f32[]{:T(128)}, f32[2,1280]{1,0:T(2,128)S(1)}) all-reduce(f32[]{:T(128)} %fusion.27, f32[2,1280]{1,0:T(2,128)S(1)} %fusion.28), channel_id=1, replica_groups=mesh['dp'=8,'expert'=4] {'expert'}, use_global_device_ids=true, to_apply=%region_11.13 | all-reduce | flops 2561 | bytes 20488 | tf_op jit(solution)/shard_map/psum | solution.py:119
  298.0 0.7 multiply_divide_fusion
  298.7 6.0 %multiply_reduce_fusion.2 = (f32[2]{0:T(128)S(1)}, f32[2,4352]{1,0:T(2,128)S(1)}) fusion(pred[2,4352]{1,0:T(4,128)(4,1)S(1)} %compare_reduce_fusion, f32[4352]{0:T(1024)S(1)} %multiply_divide_fusion, bf16[1280,4352]{1,0:T(8,128)(2,1)} %param.17, f32[2,1280]{1,0:T(2,128)S(1)} %get-tuple-element.58, f32[2]{0:T(128)S(1)} %fusion.32), kind=kOutput, calls=%fused_computation.52 | convolution fusion | flops 22496254 | bytes 11212304 | tf_op jit(solution)/shard_map/dot_general | solution.py:130
  304.7 6.0 %convolution_convert_fusion = bf16[1280,4352]{1,0:T(8,128)(2,1)} fusion(f32[2,1280]{1,0:T(2,128)S(1)} %get-tuple-element.58, f32[2]{0:T(128)S(1)} %fusion.32, pred[2,4352]{1,0:T(4,128)(4,1)S(1)} %compare_reduce_fusion, f32[2,4352]{1,0:T(2,128)S(1)} %get-tuple-element.67, f32[4352]{0:T(1024)S(1)} %multiply_divide_fusion), kind=kOutput, calls=%fused_computation.2 | convolution fusion | flops 28258304 | bytes 11212296 | tf_op jit(solution)/shard_map/dot_general | solution.py:141
  310.7 1.1 copy-done.6
  311.8 12.1 %convolution_convert_fusion.2 = bf16[1280,5120]{1,0:T(8,128)(2,1)} fusion(bf16[320,1280]{1,0:T(8,128)(2,1)S(1)} %copy-done.6, bf16[320,5120]{1,0:T(8,128)(2,1)} %copy-done.9), kind=kOutput, calls=%fused_computation.4 | convolution fusion | flops 4200857600 | bytes 17203200 | tf_op jit(solution)/shard_map/dot_general | solution.py:45
  323.9 15.5 %convolution_convert_fusion.1 = bf16[5120,1280]{1,0:T(8,128)(2,1)} fusion(bf16[320,1280]{1,0:T(8,128)(2,1)S(1)} %copy-done.4, f32[320,5120]{1,0:T(8,128)} %get-tuple-element.65), kind=kOutput, calls=%fused_computation.3 | convolution fusion | flops 4215603200 | bytes 20480000 | tf_op jit(solution)/shard_map/dot_general | solution.py:42
  339.5 3.0 fusion.35
  342.5 11.5 %all-reduce = (f32[2]{0:T(128)}, f32[2,1280]{1,0:T(2,128)S(1)}) all-reduce(f32[2]{0:T(128)S(1)} %get-tuple-element.66, f32[2,1280]{1,0:T(2,128)S(1)} %fusion.35), channel_id=1, replica_groups=mesh['dp'=8,'expert'=4] {'expert'}, use_global_device_ids=true, to_apply=%region_16.19 | all-reduce | flops 2562 | bytes 20496 | tf_op jit(solution)/shard_map/psum | solution.py:138
  353.9 0.8 reshape.152
  354.8 0.6 copy.52
  355.5 1.6 reduce_sum.144
  357.4 0.7 add_add_fusion
  358.1 0.8 add_convert_fusion
  358.9 136.5 %reduce-scatter.2.cloned.1.call-done = bf16[160,4352]{1,0:T(8,128)(2,1)} async-done(((bf16[1280,4352]{1,0:T(8,128)(2,1)}), bf16[160,4352]{1,0:T(8,128)(2,1)}) %reduce-scatter.2.cloned.1.call-update) | async-done | bytes 1392656 | tf_op jit(solution)/shard_map/reduce_scatter | solution.py:140
  (59 shorter events, 3.7 us)
Async XLA Ops:
  7.2 7.7 %copy-start.7 = (s32[128,2]{0,1:T(2,128)S(1)}, s32[128,2]{0,1:T(2,128)}, u32[]{:S(2)}) copy-start(s32[128,2]{0,1:T(2,128)} %param.12) | copy-start | bytes 3076
  77.2 17.3 %copy-start.3 = (bf16[320,1280]{1,0:T(8,128)(2,1)}, bf16[320,1280]{1,0:T(8,128)(2,1)S(1)}, u32[]{:S(2)}) copy-start(bf16[320,1280]{1,0:T(8,128)(2,1)S(1)} %reshape_squeeze.7) | copy-start | bytes 2457604
  78.9 15.5 %copy-start.5 = (bf16[320,1280]{1,0:T(8,128)(2,1)}, bf16[320,1280]{1,0:T(8,128)(2,1)S(1)}, u32[]{:S(2)}) copy-start(bf16[320,1280]{1,0:T(8,128)(2,1)S(1)} %reshape_squeeze.6) | copy-start | bytes 2457604
  107.9 1.7 copy-start.9
  118.8 63.8 %all-to-all-start.2 = ((f32[32,10,1280]{2,1,0:T(8,128)}), f32[32,10,1280]{2,1,0:T(8,128)}, u32[]{:S(2)}, u32[]{:S(2)}) async-start(f32[32,10,1280]{2,1,0:T(8,128)} %reshape.150), calls=%async_computation.2 | async-start | bytes 5242880 | tf_op jit(solution)/shard_map/all_to_all | solution.py:59
  133.8 53.2 %copy-start.8 = (s32[2,4]{1,0:T(2,128)S(1)}, s32[2,4]{1,0:T(2,128)}, u32[]{:S(2)}) copy-start(s32[2,4]{1,0:T(2,128)} %param.18) | copy-start | bytes 100
  182.6 92.5 %all-to-all-start.1 = ((f32[32,10,1280]{2,1,0:T(8,128)}), f32[32,10,1280]{2,1,0:T(8,128)}, u32[]{:S(2)}, u32[]{:S(2)}) async-start(f32[32,10,1280]{2,1,0:T(8,128)} %reshape.147), calls=%async_computation.1 | async-start | bytes 5242880 | tf_op jit(solution)/shard_map/all_to_all | solution.py:59
  186.9 308.5 %reduce-scatter.2.cloned.1.call-start = ((), (), s32[]{:S(2)}) async-start(), calls=%async_computation.4 | async-start | bytes 12533760 | tf_op jit(solution)/shard_map/reduce_scatter | solution.py:140
  279.1 6.8 %copy-start.1 = (bf16[128,1280]{1,0:T(8,128)(2,1)S(1)}, bf16[128,1280]{1,0:T(8,128)(2,1)}, u32[]{:S(2)}) copy-start(bf16[128,1280]{1,0:T(8,128)(2,1)} %param.11) | copy-start | bytes 983044
  286.0 18.7 %copy-start = (bf16[128,1280]{1,0:T(8,128)(2,1)}, bf16[128,1280]{1,0:T(8,128)(2,1)S(1)}, u32[]{:S(2)}) copy-start(bf16[128,1280]{1,0:T(8,128)(2,1)S(1)} %add_convert_fusion.1) | copy-start | bytes 983044
  310.7 1.1 copy-start.6
  311.8 12.1 %copy-start.4 = (bf16[320,1280]{1,0:T(8,128)(2,1)S(1)}, bf16[320,1280]{1,0:T(8,128)(2,1)}, u32[]{:S(2)}) copy-start(bf16[320,1280]{1,0:T(8,128)(2,1)} %copy-done.3) | copy-start | bytes 2457604
  311.8 27.6 %slice-start = ((s8[11141120]{0:T(1024)(128)(4,1)}), s8[4194304]{0:T(1024)(128)(4,1)S(1)}, s32[]{:S(2)}) async-start(s8[11141120]{0:T(1024)(128)(4,1)} %bitcast.34), calls=%async_computation.5 | async-start | bytes 8388608
  311.8 27.6 %slice-start.1 = ((s8[11141120]{0:T(1024)(128)(4,1)}), s8[4194304]{0:T(1024)(128)(4,1)S(1)}, s32[]{:S(2)}) async-start(s8[11141120]{0:T(1024)(128)(4,1)} %bitcast.34), calls=%async_computation.6 | async-start | bytes 8388608
  323.9 15.5 %slice-start.2 = ((s8[11141120]{0:T(1024)(128)(4,1)}), s8[2752512]{0:T(1024)(128)(4,1)S(1)}, s32[]{:S(2)}) async-start(s8[11141120]{0:T(1024)(128)(4,1)} %bitcast.34), calls=%async_computation.7 | async-start | bytes 5505024
  339.4 18.7 %copy-start.2 = (bf16[128,1280]{1,0:T(8,128)(2,1)S(1)}, bf16[128,1280]{1,0:T(8,128)(2,1)}, u32[]{:S(2)}) copy-start(bf16[128,1280]{1,0:T(8,128)(2,1)} %param.16) | copy-start | bytes 983044
Sparse Core Ops, SparseCore 0:
  310.8 184.5 reduce-scatter.1
where the time goes:
time: 508 us; the launch traced here: 502 us
  waiting for transfers between devices  184 us (36%)
  blocking collectives  152 us (30%)
  matrix products  92.5 us (18%)
  local copies, waits for them, and re-layouts  38.8 us (8%)
  between operations  14.6 us (3%)
  other arithmetic  12.5 us (2%)
  starting transfers between devices  7.92 us (2%)
    reduce_scatter x1, waiting for transfers between devices, shards(): lax.psum_scatter(lax.dot_general(normed_bf, d_logits, (((0,), (0,)), ((),...  136 us
    psum x1, blocking collectives, shards(): counts = lax.psum(jnp.sum(targets, axis=0), 'dp')  83 us
    all_to_all x2, waiting for transfers between devices, to_sources(): lax.all_to_all(partials, ('dp', 'expert'), split_axis=0, concat_axis=0, t...  47.1 us
    all_to_all x1, blocking collectives, to_experts(): lax.all_to_all(stacked, ('dp', 'expert'), split_axis=1, concat_axis=1, ti...  46.5 us
    dot_general x1, matrix products, expert_pass(): lax.dot_general(grad_rows, w_second, (((1,), (1,)), ((), ())), preferred_...  15.5 us
    dot_general x1, matrix products, expert_pass(): lax.dot_general(hidden_bf, grad_rows, (((0,), (0,)), ((), ())), preferred...  15.5 us
    dot_general x1, matrix products, expert_pass(): h_pre = jnp.dot(xs_rows, w_first, preferred_element_type=jnp.float32)  13.4 us
    dot_general x1, matrix products, expert_pass(): lax.dot_general(xs_rows, d_pre, (((0,), (0,)), ((), ())), preferred_eleme...  12.1 us
  transfers between devices with their start and end apart: 3, of which 2 were waited for; matrix products, arithmetic and copies ran while one was open for 11% of the time, Pallas kernels for 0%

commit v1 on v0

v1 whole, which is shorter than its diff:
```python
import jax
import jax.numpy as jnp
from jax import lax
from jax.sharding import PartitionSpec as P

D = 1280
EXPERTS = 32
PATCHES = 256
CLASSES = 17408


beta_rate = 0.99
norm_eps = 1e-06


def gelu_fn(values):
    return jax.nn.gelu(values, approximate=True)


def normalize(pooled):
    center = jnp.mean(pooled, axis=1, keepdims=True)
    spread = jnp.mean(jnp.square(pooled - center), axis=1, keepdims=True)
    return (pooled - center) * lax.rsqrt(spread + norm_eps)


def weighted_focal(logit_vals, targets, class_weight):
    nll_vals = targets * jax.nn.softplus(-logit_vals) + (1.0 - targets) * jax.nn.softplus(
        logit_vals
    )
    return class_weight[None, :] * jnp.square(1.0 - jnp.exp(-nll_vals)) * nll_vals


def swap(messages):
    return lax.all_to_all(messages, ("dp", "expert"), split_axis=0, concat_axis=0, tiled=True)


def pack(rows, n_devices):
    return rows.reshape(n_devices, -1, 128)


def unpack(messages):
    return messages.reshape(-1, D)


def contract_last(left, right):
    return lax.dot_general(left, right, (((1,), (1,)), ((), ())), preferred_element_type=jnp.float32)


def contract_first(left, right):
    return lax.dot_general(left, right, (((0,), (0,)), ((), ())), preferred_element_type=jnp.float32)


def share_out(rows, capacity, share_count):
    rows = rows.reshape(EXPERTS, 1, capacity, D)
    return jnp.broadcast_to(rows, (EXPERTS, share_count, capacity, D)).reshape(-1, D)


def shards(tokens, routes, combine, w_in, w_out, out_grad, head_w, labels):
    dp_size = lax.axis_size("dp")
    ex_size = lax.axis_size("expert")
    n_devices = dp_size * ex_size
    tok_rows = tokens.shape[0]
    capacity = 5 * tok_rows // 64
    share_count = n_devices // EXPERTS
    buffer_rows = EXPERTS * capacity
    ex_index = lax.axis_index("expert")
    dp_index = lax.axis_index("dp")

    flat_routes = routes.reshape(tok_rows * 2)
    route_hits = (flat_routes[:, None] == jnp.arange(EXPERTS, dtype=jnp.int32)[None, :]).astype(
        jnp.int32
    )
    earlier = jnp.cumsum(route_hits, axis=0) - route_hits
    slot_pos = jnp.sum(earlier * route_hits, axis=1)
    slot_index = flat_routes * capacity + slot_pos
    pair_table = (jnp.arange(buffer_rows, dtype=jnp.int32)[:, None] == slot_index[None, :]).astype(
        jnp.bfloat16
    )
    token_table = jnp.sum(pair_table.reshape(buffer_rows, tok_rows, 2), axis=2)
    pair_grad = (
        (combine[:, :, None] * out_grad.astype(jnp.float32)[:, None, :])
        .astype(jnp.bfloat16)
        .reshape(tok_rows * 2, D)
    )
    x_buf = jnp.dot(token_table, tokens, preferred_element_type=jnp.float32).astype(jnp.bfloat16)
    g_buf = jnp.dot(pair_table, pair_grad, preferred_element_type=jnp.float32).astype(jnp.bfloat16)
    x_msg = pack(share_out(x_buf, capacity, share_count), n_devices)
    g_msg = pack(share_out(g_buf, capacity, share_count), n_devices)

    class_cols = head_w.shape[1]
    all_labels = lax.all_gather(labels, "dp", axis=0, tiled=True)
    all_ids = jnp.arange(CLASSES, dtype=jnp.int32)
    counts = jnp.sum(
        jnp.any(all_labels[:, :, None] == all_ids[None, None, :], axis=1).astype(jnp.float32), axis=0
    )
    effective = (1.0 - beta_rate) / (1.0 - jnp.power(beta_rate, counts + 1.0))
    all_weight = effective * CLASSES / jnp.sum(effective)
    class_weight = lax.dynamic_slice_in_dim(all_weight, ex_index * class_cols, class_cols)
    class_ids = ex_index * class_cols + jnp.arange(class_cols, dtype=jnp.int32)
    targets = jnp.any(labels[:, :, None] == class_ids[None, None, :], axis=1).astype(jnp.float32)

    x_in = swap(x_msg)
    x_in, g_msg = lax.optimization_barrier((x_in, g_msg))
    g_in = swap(g_msg)
    xs_rows = unpack(x_in)
    h_pre = jnp.dot(xs_rows, w_in, preferred_element_type=jnp.float32)
    hidden, gelu_back = jax.vjp(gelu_fn, h_pre)
    hidden_bf = hidden.astype(jnp.bfloat16)
    expert_out = jnp.dot(hidden_bf, w_out, preferred_element_type=jnp.float32).astype(jnp.bfloat16)
    out_msg = pack(expert_out, n_devices)
    out_msg, g_in = lax.optimization_barrier((out_msg, g_in))
    back_out = swap(out_msg)

    grad_rows = unpack(g_in)
    d_hidden = contract_last(grad_rows, w_out)
    d_pre = gelu_back(d_hidden)[0].astype(jnp.bfloat16)
    d_rows = contract_last(d_pre, w_in).astype(jnp.bfloat16)
    rows_msg = pack(d_rows, n_devices)
    rows_msg, d_pre, hidden_bf = lax.optimization_barrier((rows_msg, d_pre, hidden_bf))
    back_rows = swap(rows_msg)
    d_w_out = contract_first(hidden_bf, grad_rows).astype(jnp.bfloat16)
    d_w_in = contract_first(xs_rows, d_pre).astype(jnp.bfloat16)

    def collect(messages):
        rows = unpack(messages).reshape(EXPERTS, share_count, capacity, D)
        rows = jnp.sum(rows.astype(jnp.float32), axis=1).reshape(buffer_rows, D)
        return contract_first(pair_table, rows.astype(jnp.bfloat16)).reshape(tok_rows, 2, D) if (
            share_count == 1
        ) else jnp.take(rows, slot_index, axis=0).reshape(tok_rows, 2, D)

    expert_vals = collect(back_out)
    mixed_out = (
        tokens.astype(jnp.float32) + jnp.sum(combine[:, :, None] * expert_vals, axis=1)
    ).astype(jnp.bfloat16)
    d_combine = jnp.sum(out_grad.astype(jnp.float32)[:, None, :] * expert_vals, axis=2)

    images = labels.shape[0]
    token_image = (ex_index * tok_rows + jnp.arange(tok_rows, dtype=jnp.int32)) // PATCHES
    mixed_f32 = mixed_out.astype(jnp.float32)
    pooled_part = jnp.stack(
        [
            jnp.sum(jnp.where((token_image == image)[:, None], mixed_f32, 0.0), axis=0)
            for image in range(images)
        ]
    )
    pooled = lax.psum(pooled_part, "expert") / PATCHES
    normed, norm_back = jax.vjp(normalize, pooled)
    normed_bf = normed.astype(jnp.bfloat16)
    logits = jnp.dot(normed_bf, head_w, preferred_element_type=jnp.float32)
    focal_terms, focal_back = jax.vjp(
        lambda logit_vals: weighted_focal(logit_vals, targets, class_weight), logits
    )
    d_logits = focal_back(jnp.ones_like(focal_terms))[0].astype(jnp.bfloat16)
    pairs = lax.all_gather(
        jnp.concatenate([normed_bf, d_logits], axis=1), "dp", axis=0, tiled=True
    )
    normed_part = contract_last(d_logits, head_w)
    d_normed, image_loss = lax.psum((normed_part, jnp.sum(focal_terms, axis=1)), "expert")
    d_pooled = norm_back(d_normed)[0]
    head_rows = D // dp_size
    own_normed = lax.dynamic_slice_in_dim(pairs[:, :D], dp_index * head_rows, head_rows, axis=1)
    d_head = contract_first(own_normed, pairs[:, D:]).astype(jnp.bfloat16)

    expert_back = collect(back_rows)
    d_tokens = (out_grad.astype(jnp.float32) + jnp.sum(expert_back, axis=1)).astype(jnp.bfloat16)
    return (mixed_out, d_tokens, d_combine, d_w_in, d_w_out, image_loss, d_pooled, d_head)


def solution(mesh):
    in_specs = (
        P(("dp", "expert"), None),
        P(("dp", "expert"), None),
        P(("dp", "expert"), None),
        P(None, ("dp", "expert")),
        P(("dp", "expert"), None),
        P(("dp", "expert"), None),
        P(None, "expert"),
        P("dp", None),
    )
    out_specs = (
        P(("dp", "expert"), None),
        P(("dp", "expert"), None),
        P(("dp", "expert"), None),
        P(None, ("dp", "expert")),
        P(("dp", "expert"), None),
        P("dp"),
        P("dp", None),
        P("dp", "expert"),
    )
    return jax.shard_map(shards, mesh=mesh, in_specs=in_specs, out_specs=out_specs, check_vma=False)
```

time: 508 us -> 211 us (0.42); the launches traced: 502 us -> 211 us
  waiting for transfers between devices: 184 us -> 0.01 us
  blocking collectives: 152 us -> 75.4 us
  local copies, waits for them, and re-layouts: 38.8 us -> 21.4 us
  starting transfers between devices: 7.92 us -> 23.9 us
  matrix products: 92.5 us -> 78.4 us
  between operations: 14.6 us -> 1 us
    reduce_scatter x1 -> x0, waiting for transfers between devices: 136 us -> none  [shards(): lax.psum_scatter(lax.dot_general(normed_bf, d_logits, (((0,), (0,)), ((),...]
    psum x2 -> x1, blocking collectives: 94.6 us -> 12.7 us  [shards(): pooled = lax.psum(pooled_part, 'expert') / PATCHES]
    all_gather x0 -> x2, blocking collectives: none -> 52.1 us  [the longest x1 30.7 us: shards(): lax.all_gather(jnp.concatenate([normed_bf, d_logits], axis=1), 'dp', axis...]
    all_to_all x2 -> x4, waiting for transfers between devices: 47.1 us -> 0.01 us  [swap(): lax.all_to_all(messages, ('dp', 'expert'), split_axis=0, concat_axis=0, t...]
    all_to_all x1 -> x0, blocking collectives: 46.5 us -> none  [to_experts(): lax.all_to_all(stacked, ('dp', 'expert'), split_axis=1, concat_axis=1, ti...]
    all_to_all x2 -> x4, starting transfers between devices: 7.88 us -> 23.9 us  [swap(): lax.all_to_all(messages, ('dp', 'expert'), split_axis=0, concat_axis=0, t...]
    dot_general x9 -> x10, matrix products: 84.7 us -> 69.8 us  [the longest x5 27.4 us: contract_first(): lax.dot_general(left, right, (((0,), (0,)), ((), ())), preferred_element_...]
    slice x2, local copies, waits for them, and re-layouts: 8.57 us -> 0.19 us  [the longest x1 8.39 us: shards(): grad_rows = arrived[1].reshape(n_devices * capacity, D)]
  transfers between devices with their start and end apart: 3 -> 4, of which waited for: 2 -> 0; matrix products, arithmetic and copies ran while one was open for 11% -> 44% of each run, Pallas kernels for 0% -> 0%
where the time goes in v1:
time: 211 us
  matrix products  78.4 us (37%)
  blocking collectives  75.4 us (36%)
  starting transfers between devices  23.9 us (11%)
  local copies, waits for them, and re-layouts  21.4 us (10%)
  other arithmetic  10.5 us (5%)
    all_gather x1, blocking collectives, shards(): lax.all_gather(jnp.concatenate([normed_bf, d_logits], axis=1), 'dp', axis...  30.7 us
    dot_general x5, matrix products, contract_first(): lax.dot_general(left, right, (((0,), (0,)), ((), ())), preferred_element_...  27.4 us
    all_to_all x4, starting transfers between devices, swap(): lax.all_to_all(messages, ('dp', 'expert'), split_axis=0, concat_axis=0, t...  23.9 us
    dot_general x3, matrix products, contract_last(): lax.dot_general(left, right, (((1,), (1,)), ((), ())), preferred_element_...  22.2 us
    all_gather x1, blocking collectives, shards(): all_labels = lax.all_gather(labels, 'dp', axis=0, tiled=True)  21.4 us
    dot_general x1, matrix products, shards(): h_pre = jnp.dot(xs_rows, w_in, preferred_element_type=jnp.float32)  12.7 us
    psum x1, blocking collectives, shards(): pooled = lax.psum(pooled_part, 'expert') / PATCHES  12.7 us
    psum x1, blocking collectives, shards(): lax.psum((normed_part, jnp.sum(focal_terms, axis=1)), 'expert')  10.6 us
  transfers between devices with their start and end apart: 4, of which 0 were waited for; matrix products, arithmetic and copies ran while one was open for 44% of the time, Pallas kernels for 0%

profile of v1, /device:TPU:0, one launch (start us, length us, event | category | flops | bytes accessed | tf_op | source)
XLA Modules:
  0.0 210.5 jit_solution(13737959646303439508)
XLA Ops:
  0.6 0.8 copy.46
  1.8 0.6 reduce-window.6
  2.9 0.7 multiply_add_fusion.1
  3.7 1.3 convolution_convert_fusion.6
  5.0 1.9 reshape_reshape_reshape.6
  6.9 7.3 %all-to-all-start = ((bf16[32,100,128]{2,1,0:T(8,128)(2,1)}), bf16[32,100,128]{2,1,0:T(8,128)(2,1)S(1)}, u32[]{:S(2)}, u32[]{:S(2)}) async-start(bf16[32,100,128]{2,1,0:T(8,128)(2,1)} %reshape_reshape_reshape.6), calls=%async_computation | async-start | bytes 1703936 | tf_op jit(solution)/shard_map/all_to_all | solution.py:34
  14.2 1.9 convert_element_type.96
  16.3 0.3 copy.52
  16.6 0.3 mul.206.clone
  16.9 0.9 mul.207
  17.8 0.8 copy.50
  18.8 1.1 convolution_convert_fusion.5
  19.9 1.9 reshape_reshape_reshape.7
  21.8 21.4 %all-gather = s32[8,2,4]{2,1,0:T(2,128)S(1)} all-gather(s32[1,2,4]{2,1,0:T(2,128)} %bitcast.48), channel_id=1, replica_groups=mesh['dp'=8,'expert'=4] {'dp'}, dimensions={0}, use_global_device_ids=true | all-gather | bytes 288 | tf_op jit(solution)/shard_map/all_gather | solution.py:91
  43.3 1.3 fusion.7
  44.6 0.2 convert_reduce_fusion
  44.9 0.6 fusion.32
  45.5 0.7 fusion.28
  46.2 0.9 compare_reduce_fusion
  47.1 0.9 reshape.186
  48.0 5.0 %all-to-all-start.1 = ((bf16[32,100,128]{2,1,0:T(8,128)(2,1)}), bf16[32,100,128]{2,1,0:T(8,128)(2,1)S(1)}, u32[]{:S(2)}, u32[]{:S(2)}) async-start(bf16[32,100,128]{2,1,0:T(8,128)(2,1)} %reshape_reshape_reshape.7), calls=%async_computation.1 | async-start | bytes 1703936 | tf_op jit(solution)/shard_map/all_to_all | solution.py:34
  53.0 12.7 %multiply_convert_fusion = (bf16[320,5120]{1,0:T(8,128)(2,1)S(1)}, f32[320,5120]{1,0:T(8,128)}) fusion(bf16[320,1280]{1,0:T(8,128)(2,1)S(1)} %reshape.186, bf16[1280,5120]{1,0:T(8,128)(2,1)} %param.12), kind=kOutput, calls=%fused_computation.11 | convolution fusion | flops 4209049600 | bytes 23756800 | tf_op jit(solution)/shard_map/dot_general | solution.py:106
  65.7 1.7 copy-done.8
  67.4 7.5 %convolution_convert_fusion.4 = bf16[320,1280]{1,0:T(8,128)(2,1)S(1)} fusion(bf16[320,5120]{1,0:T(8,128)(2,1)S(1)} %get-tuple-element.25, bf16[5120,1280]{1,0:T(8,128)(2,1)} %param.13), kind=kOutput, calls=%fused_computation.16 | convolution fusion | flops 4194713600 | bytes 17203200 | tf_op jit(solution)/shard_map/dot_general | solution.py:109
  74.9 1.9 reshape.187
  76.8 5.9 %all-to-all-start.2 = ((bf16[32,100,128]{2,1,0:T(8,128)(2,1)}), bf16[32,100,128]{2,1,0:T(8,128)(2,1)S(1)}, u32[]{:S(2)}, u32[]{:S(2)}) async-start(bf16[32,100,128]{2,1,0:T(8,128)(2,1)} %reshape.187), calls=%async_computation.2 | async-start | bytes 1703936 | tf_op jit(solution)/shard_map/all_to_all | solution.py:34
  82.7 0.9 reshape.188
  83.6 11.6 %fusion.6 = bf16[320,5120]{1,0:T(8,128)(2,1)S(1)} fusion(f32[320,5120]{1,0:T(8,128)} %get-tuple-element.46, bf16[320,1280]{1,0:T(8,128)(2,1)S(1)} %reshape.188, bf16[5120,1280]{1,0:T(8,128)(2,1)} %param.13), kind=kOutput, calls=%fused_computation.10 | convolution fusion | flops 4227072000 | bytes 23756800 | tf_op jit(solution)/shard_map/dot_general | solution.py:46
  95.2 1.7 copy-done.7
  96.9 7.6 %convolution_convert_fusion.3 = bf16[320,1280]{1,0:T(8,128)(2,1)S(1)} fusion(bf16[320,5120]{1,0:T(8,128)(2,1)S(1)} %fusion.6, bf16[1280,5120]{1,0:T(8,128)(2,1)} %param.12), kind=kOutput, calls=%fused_computation.15 | convolution fusion | flops 4194713600 | bytes 17203200 | tf_op jit(solution)/shard_map/dot_general | solution.py:46
  104.5 1.9 reshape.189
  106.4 12.1 %convolution_convert_fusion.1 = bf16[1280,5120]{1,0:T(8,128)(2,1)} fusion(bf16[320,1280]{1,0:T(8,128)(2,1)S(1)} %reshape.186, bf16[320,5120]{1,0:T(8,128)(2,1)} %copy-done.7), kind=kOutput, calls=%fused_computation.1 | convolution fusion | flops 4200857600 | bytes 17203200 | tf_op jit(solution)/shard_map/dot_general | solution.py:50
  118.5 10.3 %convolution_convert_fusion = bf16[5120,1280]{1,0:T(8,128)(2,1)} fusion(bf16[320,5120]{1,0:T(8,128)(2,1)S(1)} %copy-done.9, bf16[320,1280]{1,0:T(8,128)(2,1)S(1)} %copy-done.4), kind=kOutput, calls=%fused_computation | convolution fusion | flops 4200857600 | bytes 17203200 | tf_op jit(solution)/shard_map/dot_general | solution.py:50
  128.8 5.7 %all-to-all-start.3 = ((bf16[32,100,128]{2,1,0:T(8,128)(2,1)}), bf16[32,100,128]{2,1,0:T(8,128)(2,1)}, u32[]{:S(2)}, u32[]{:S(2)}) async-start(bf16[32,100,128]{2,1,0:T(8,128)(2,1)} %reshape.189), calls=%async_computation.3 | async-start | bytes 1703936 | tf_op jit(solution)/shard_map/all_to_all | solution.py:34
  134.6 1.8 reshape.194
  136.4 2.7 %multiply_reduce_fusion = (f32[128,2]{0,1:T(2,128)}, f32[128,1280]{1,0:T(8,128)S(1)}) fusion(f32[128,1280]{1,0:T(8,128)} %convert_element_type.96, f32[128,2]{0,1:T(2,128)S(1)} %copy-done.6, pred[128,2,320]{0,2,1:T(32,128)(4,1)S(1)} %copy.52, bf16[320,1280,1]{1,0,2:T(8,128)(2,1)} %reshape.194), kind=kOutput, calls=%fused_computation.20 | convolution fusion | flops 210861824 | bytes 2213888 | tf_op jit(solution)/shard_map/dot_general | solution.py:50
  139.1 0.9 fusion.8
  140.1 12.7 %psum.21 = f32[2,1280]{1,0:T(2,128)S(1)} all-reduce(f32[2,1280]{1,0:T(2,128)S(1)} %pad_maximum_fusion), channel_id=1, replica_groups=mesh['dp'=8,'expert'=4] {'expert'}, use_global_device_ids=true, to_apply=%region_13.14 | all-reduce | flops 2560 | bytes 20480 | tf_op jit(solution)/shard_map/psum | solution.py:146
  153.2 6.1 %fusion.23 = (bf16[2,4352]{1,0:T(2,128)(2,1)S(1)}, f32[2]{0:T(128)S(1)}) fusion(pred[2,4352]{1,0:T(4,128)(4,1)S(1)} %compare_reduce_fusion, f32[4352]{0:T(1024)S(1)} %fusion.28, bf16[2,1280]{1,0:T(2,128)(2,1)S(1)} %multiply_convert_fusion.3, bf16[1280,4352]{1,0:T(8,128)(2,1)} %param.15), kind=kOutput, calls=%fused_computation.59 | convolution fusion | flops 22700030 | bytes 11189768 | tf_op jit(solution)/shard_map/dot_general | solution.py:149
  159.3 0.5 slice-done.2
  159.8 3.0 %fusion.33 = f32[2,1280]{1,0:T(2,128)S(1)} fusion(bf16[2,4352]{1,0:T(2,128)(2,1)S(1)} %get-tuple-element.43, bf16[1280,4352]{1,0:T(8,128)(2,1)S(1)} %bitcast.46), kind=kOutput, calls=%fused_computation.98 | convolution fusion | flops 22282240 | bytes 11168768 | tf_op jit(solution)/shard_map/dot_general | solution.py:46
  162.9 2.1 reshape.195
  165.0 0.5 convolution_reduce_fusion
  165.5 0.8 add_convert_fusion
  166.3 10.6 %all-reduce = (f32[2]{0:T(128)}, f32[2,1280]{1,0:T(2,128)S(1)}) all-reduce(f32[2]{0:T(128)S(1)} %get-tuple-element.44, f32[2,1280]{1,0:T(2,128)S(1)} %fusion.33), channel_id=1, replica_groups=mesh['dp'=8,'expert'=4] {'expert'}, use_global_device_ids=true, to_apply=%region_17.19 | all-reduce | flops 2562 | bytes 20496 | tf_op jit(solution)/shard_map/psum | solution.py:158
  177.3 0.7 add_add_fusion
  178.0 30.7 %all-gather.1 = bf16[8,2,5632]{2,1,0:T(2,128)(2,1)S(1)} all-gather(bf16[1,2,5632]{2,1,0:T(2,128)(2,1)S(1)} %maximum_bitcast_fusion), channel_id=1, replica_groups=mesh['dp'=8,'expert'=4] {'dp'}, dimensions={0}, use_global_device_ids=true | all-gather | bytes 202752 | tf_op jit(solution)/shard_map/all_gather | solution.py:154
  208.8 1.7 convolution_convert_fusion.2
  (60 shorter events, 2.4 us)
Async XLA Ops:
  0.6 15.9 %copy-start = (bf16[128,1280]{1,0:T(8,128)(2,1)S(1)}, bf16[128,1280]{1,0:T(8,128)(2,1)}, u32[]{:S(2)}) copy-start(bf16[128,1280]{1,0:T(8,128)(2,1)} %param.14) | copy-start | bytes 983044
  6.9 40.2 %all-to-all-start = ((bf16[32,100,128]{2,1,0:T(8,128)(2,1)}), bf16[32,100,128]{2,1,0:T(8,128)(2,1)S(1)}, u32[]{:S(2)}, u32[]{:S(2)}) async-start(bf16[32,100,128]{2,1,0:T(8,128)(2,1)} %reshape_reshape_reshape.6), calls=%async_computation | async-start | bytes 1703936 | tf_op jit(solution)/shard_map/all_to_all | solution.py:34
  14.2 1.9 copy-start.5
  48.0 28.7 %all-to-all-start.1 = ((bf16[32,100,128]{2,1,0:T(8,128)(2,1)}), bf16[32,100,128]{2,1,0:T(8,128)(2,1)S(1)}, u32[]{:S(2)}, u32[]{:S(2)}) async-start(bf16[32,100,128]{2,1,0:T(8,128)(2,1)} %reshape_reshape_reshape.7), calls=%async_computation.1 | async-start | bytes 1703936 | tf_op jit(solution)/shard_map/all_to_all | solution.py:34
  65.7 1.7 copy-start.8
  76.8 52.1 %all-to-all-start.2 = ((bf16[32,100,128]{2,1,0:T(8,128)(2,1)}), bf16[32,100,128]{2,1,0:T(8,128)(2,1)S(1)}, u32[]{:S(2)}, u32[]{:S(2)}) async-start(bf16[32,100,128]{2,1,0:T(8,128)(2,1)} %reshape.187), calls=%async_computation.2 | async-start | bytes 1703936 | tf_op jit(solution)/shard_map/all_to_all | solution.py:34
  83.6 11.6 %copy-start.3 = (bf16[320,1280]{1,0:T(8,128)(2,1)}, bf16[320,1280]{1,0:T(8,128)(2,1)S(1)}, u32[]{:S(2)}) copy-start(bf16[320,1280]{1,0:T(8,128)(2,1)S(1)} %reshape.188) | copy-start | bytes 2457604
  95.2 1.7 copy-start.7
  106.4 12.1 %copy-start.4 = (bf16[320,1280]{1,0:T(8,128)(2,1)S(1)}, bf16[320,1280]{1,0:T(8,128)(2,1)}, u32[]{:S(2)}) copy-start(bf16[320,1280]{1,0:T(8,128)(2,1)} %copy-done.3) | copy-start | bytes 2457604
  106.4 12.1 %copy-start.9 = (bf16[320,5120]{1,0:T(8,128)(2,1)S(1)}, bf16[320,5120]{1,0:T(8,128)(2,1)}, u32[]{:S(2)}) copy-start(bf16[320,5120]{1,0:T(8,128)(2,1)} %copy-done.8) | copy-start | bytes 9830404
  118.5 17.9 %copy-start.6 = (f32[128,2]{0,1:T(2,128)S(1)}, f32[128,2]{0,1:T(2,128)}, u32[]{:S(2)}) copy-start(f32[128,2]{0,1:T(2,128)} %param.11) | copy-start | bytes 3076
  118.5 20.6 %copy-start.2 = (bf16[128,1280]{1,0:T(8,128)(2,1)S(1)}, bf16[128,1280]{1,0:T(8,128)(2,1)}, u32[]{:S(2)}) copy-start(bf16[128,1280]{1,0:T(8,128)(2,1)} %param.9) | copy-start | bytes 983044
  128.8 34.0 %all-to-all-start.3 = ((bf16[32,100,128]{2,1,0:T(8,128)(2,1)}), bf16[32,100,128]{2,1,0:T(8,128)(2,1)}, u32[]{:S(2)}, u32[]{:S(2)}) async-start(bf16[32,100,128]{2,1,0:T(8,128)(2,1)} %reshape.189), calls=%async_computation.3 | async-start | bytes 1703936 | tf_op jit(solution)/shard_map/all_to_all | solution.py:34
  136.4 22.9 %slice-start = ((s8[11141120]{0:T(1024)(128)(4,1)}), s8[2752512]{0:T(1024)(128)(4,1)S(1)}, s32[]{:S(2)}) async-start(s8[11141120]{0:T(1024)(128)(4,1)} %bitcast.45), calls=%async_computation.4 | async-start | bytes 5505024
  153.2 6.1 %slice-start.1 = ((s8[11141120]{0:T(1024)(128)(4,1)}), s8[4194304]{0:T(1024)(128)(4,1)S(1)}, s32[]{:S(2)}) async-start(s8[11141120]{0:T(1024)(128)(4,1)} %bitcast.45), calls=%async_computation.5 | async-start | bytes 8388608
  153.2 6.6 %slice-start.2 = ((s8[11141120]{0:T(1024)(128)(4,1)}), s8[4194304]{0:T(1024)(128)(4,1)S(1)}, s32[]{:S(2)}) async-start(s8[11141120]{0:T(1024)(128)(4,1)} %bitcast.45), calls=%async_computation.6 | async-start | bytes 8388608
  159.8 5.7 %copy-start.1 = (bf16[128,1280]{1,0:T(8,128)(2,1)S(1)}, bf16[128,1280]{1,0:T(8,128)(2,1)}, u32[]{:S(2)}) copy-start(bf16[128,1280]{1,0:T(8,128)(2,1)} %param.14) | copy-start | bytes 983044

commit v2 on v1

--- a/solution.py
+++ b/solution.py
@@ -1,6 +1,10 @@
+import functools
+
 import jax
 import jax.numpy as jnp
 from jax import lax
+from jax.experimental import pallas as pl
+from jax.experimental.pallas import tpu as pltpu
 from jax.sharding import PartitionSpec as P
 
 D = 1280
@@ -53,6 +57,61 @@
 def share_out(rows, capacity, share_count):
     rows = rows.reshape(EXPERTS, 1, capacity, D)
     return jnp.broadcast_to(rows, (EXPERTS, share_count, capacity, D)).reshape(-1, D)
+
+
+def gather_kernel(axes, *refs):
+    count = len(axes)
+    sources, results = refs[:count], refs[count : 2 * count]
+    send_sems, recv_sems = refs[2 * count : 3 * count], refs[3 * count :]
+    partners = [
+        (axis, shift, lax.rem(lax.axis_index(axis) + shift, lax.axis_size(axis)))
+        for axis in axes
+        for shift in range(1, lax.axis_size(axis))
+    ]
+    barrier = pltpu.get_barrier_semaphore()
+    for axis, _, peer in partners:
+        pl.semaphore_signal(
+            barrier, inc=1, device_id={axis: peer}, device_id_type=pl.DeviceIdType.MESH
+        )
+    pl.semaphore_wait(barrier, len(partners))
+    copies = []
+    for axis, shift, peer in partners:
+        item = axes.index(axis)
+        copy = pltpu.make_async_remote_copy(
+            src_ref=sources[item],
+            dst_ref=results[item].at[lax.axis_index(axis)],
+            send_sem=send_sems[item].at[shift],
+            recv_sem=recv_sems[item].at[shift],
+            device_id={axis: peer},
+            device_id_type=pl.DeviceIdType.MESH,
+        )
+        copy.start()
+        copies.append(copy)
+    for axis, source, result in zip(axes, sources, results):
+        result[lax.axis_index(axis)] = source[...]
+    for copy in copies:
+        copy.wait()
+
+
+def gather(arrays, axes, collective_id):
+    sizes = [lax.axis_size(axis) for axis in axes]
+    moved = sum(size * array.size * 4 for size, array in zip(sizes, arrays))
+    return pl.pallas_call(
+        functools.partial(gather_kernel, axes),
+        out_shape=[
+            jax.ShapeDtypeStruct((size,) + array.shape, array.dtype)
+            for size, array in zip(sizes, arrays)
+        ],
+        in_specs=[pl.BlockSpec(memory_space=pltpu.VMEM)] * len(axes),
+        out_specs=[pl.BlockSpec(memory_space=pltpu.VMEM)] * len(axes),
+        scratch_shapes=[pltpu.SemaphoreType.DMA((size,)) for size in sizes] * 2,
+        compiler_params=pltpu.CompilerParams(
+            collective_id=collective_id,
+            has_side_effects=True,
+            vmem_limit_bytes=8 * 1024 * 1024,
+        ),
+        cost_estimate=pl.CostEstimate(flops=0, bytes_accessed=moved, transcendentals=0),
+    )(*arrays)
 
 
 def shards(tokens, routes, combine, w_in, w_out, out_grad, head_w, labels):
@@ -88,7 +147,11 @@
     g_msg = pack(share_out(g_buf, capacity, share_count), n_devices)
 
     class_cols = head_w.shape[1]
-    all_labels = lax.all_gather(labels, "dp", axis=0, tiled=True)
+    label_rows, label_count = labels.shape
+    label_block = jnp.pad(labels, ((0, -label_rows % 8), (0, 128 - label_count)))
+    label_block, g_msg = lax.optimization_barrier((label_block, g_msg))
+    (all_labels,) = gather([label_block], ("dp",), 0)
+    all_labels = all_labels[:, :label_rows, :label_count].reshape(-1, label_count)
     all_ids = jnp.arange(CLASSES, dtype=jnp.int32)
     counts = jnp.sum(
         jnp.any(all_labels[:, :, None] == all_ids[None, None, :], axis=1).astype(jnp.float32), axis=0
@@ -143,7 +206,8 @@
             for image in range(images)
         ]
     )
-    pooled = lax.psum(pooled_part, "expert") / PATCHES
+    (pooled_parts,) = gather([pooled_part], ("expert",), 1)
+    pooled = jnp.sum(pooled_parts, axis=0) / PATCHES
     normed, norm_back = jax.vjp(normalize, pooled)
     normed_bf = normed.astype(jnp.bfloat16)
     logits = jnp.dot(normed_bf, head_w, preferred_element_type=jnp.float32)
@@ -151,11 +215,19 @@
         lambda logit_vals: weighted_focal(logit_vals, targets, class_weight), logits
     )
     d_logits = focal_back(jnp.ones_like(focal_terms))[0].astype(jnp.bfloat16)
-    pairs = lax.all_gather(
-        jnp.concatenate([normed_bf, d_logits], axis=1), "dp", axis=0, tiled=True
-    )
     normed_part = contract_last(d_logits, head_w)
-    d_normed, image_loss = lax.psum((normed_part, jnp.sum(focal_terms, axis=1)), "expert")
+    loss_part = jnp.broadcast_to(jnp.sum(focal_terms, axis=1)[:, None], (images, 128))
+    pairs, parts = gather(
+        [
+            jnp.concatenate([normed_bf, d_logits], axis=1).astype(jnp.float32),
+            jnp.concatenate([normed_part, loss_part], axis=1),
+        ],
+        ("dp", "expert"),
+        2,
+    )
+    pairs = pairs.reshape(-1, D + class_cols).astype(jnp.bfloat16)
+    parts = jnp.sum(parts, axis=0)
+    d_normed, image_loss = parts[:, :D], parts[:, D]
     d_pooled = norm_back(d_normed)[0]
     head_rows = D // dp_size
     own_normed = lax.dynamic_slice_in_dim(pairs[:, :D], dp_index * head_rows, head_rows, axis=1)

time: 211 us -> 166 us (0.79)
  blocking collectives: 75.4 us -> 0 us
  Pallas kernels: 0 us -> 32.9 us
    all_gather x2 -> x0, blocking collectives: 52.1 us -> none  [the longest x1 30.7 us: shards(): lax.all_gather(jnp.concatenate([normed_bf, d_logits], axis=1), 'dp', axis...]
    pallas_call x0 -> x3, Pallas kernels: none -> 32.9 us  [gather(): pl.pallas_call(functools.partial(gather_kernel, axes), out_shape=[jax.Sha...]
    psum x2 -> x0, blocking collectives: 23.3 us -> none  [the longest x1 12.7 us: shards(): pooled = lax.psum(pooled_part, 'expert') / PATCHES]
  transfers between devices with their start and end apart: 4 -> 4, of which waited for: 0 -> 0; matrix products, arithmetic and copies ran while one was open for 44% -> 56% of each run, Pallas kernels for 0% -> 20%
where the time goes in v2:
time: 166 us
  matrix products  77.7 us (47%)
  Pallas kernels  32.9 us (20%)
  local copies, waits for them, and re-layouts  22 us (13%)
  starting transfers between devices  21.9 us (13%)
  other arithmetic  10 us (6%)
    pallas_call x3, Pallas kernels, gather(): pl.pallas_call(functools.partial(gather_kernel, axes), out_shape=[jax.Sha...  32.9 us
    dot_general x5, matrix products, contract_first(): lax.dot_general(left, right, (((0,), (0,)), ((), ())), preferred_element_...  27.4 us
    dot_general x3, matrix products, contract_last(): lax.dot_general(left, right, (((1,), (1,)), ((), ())), preferred_element_...  22.2 us
    all_to_all x4, starting transfers between devices, swap(): lax.all_to_all(messages, ('dp', 'expert'), split_axis=0, concat_axis=0, t...  21.9 us
    dot_general x1, matrix products, shards(): h_pre = jnp.dot(xs_rows, w_in, preferred_element_type=jnp.float32)  12.7 us
    dot_general x1, matrix products, shards(): jnp.dot(hidden_bf, w_out, preferred_element_type=jnp.float32)  7.53 us
    dot_general x1, matrix products, shards(): logits = jnp.dot(normed_bf, head_w, preferred_element_type=jnp.float32)  6.13 us
    unnamed x30, local copies, waits for them, and re-layouts  4.86 us
  transfers between devices with their start and end apart: 4, of which 0 were waited for; matrix products, arithmetic and copies ran while one was open for 56% of the time, Pallas kernels for 20%

profile of v2, /device:TPU:0, one launch (start us, length us, event | category | flops | bytes accessed | tf_op | source)
XLA Modules:
  0.0 165.6 jit_solution(6668990225727216314)
XLA Ops:
  0.7 0.8 copy.37
  1.8 0.6 reduce-window.6
  2.9 0.7 multiply_add_fusion.1
  3.7 1.3 convolution_convert_fusion.6
  5.0 1.9 %reshape_reshape_reshape.6 = bf16[32,100,128]{2,1,0:T(8,128)(2,1)} reshape(bf16[320,1280]{1,0:T(8,128)(2,1)S(1)} %convolution_convert_fusion.6) | data formatting | bytes 1638400 | tf_op jit(solution)/shard_map/reshape;reshape;reshape | solution.py:42
  6.9 7.3 %all-to-all-start = ((bf16[32,100,128]{2,1,0:T(8,128)(2,1)}), bf16[32,100,128]{2,1,0:T(8,128)(2,1)S(1)}, u32[]{:S(2)}, u32[]{:S(2)}) async-start(bf16[32,100,128]{2,1,0:T(8,128)(2,1)} %reshape_reshape_reshape.6), calls=%async_computation | async-start | bytes 1703936 | tf_op jit(solution)/shard_map/all_to_all | solution.py:38
  14.2 1.9 %convert_element_type.105 = f32[128,1280]{1,0:T(8,128)} convert(bf16[128,1280]{1,0:T(8,128)(2,1)} %param.14) | non-fusion elementwise | flops 163840 | bytes 983040 | tf_op jit(solution)/shard_map/convert_element_type | solution.py:140
  16.3 0.9 copy.43
  17.2 0.3 mul.206.clone
  17.6 0.9 mul.207
  18.7 0.5 convolution_convert_fusion.5
  19.2 1.9 %reshape_reshape_reshape.7 = bf16[32,100,128]{2,1,0:T(8,128)(2,1)} reshape(bf16[320,1280]{1,0:T(8,128)(2,1)S(1)} %convolution_convert_fusion.5) | data formatting | bytes 1638400 | tf_op jit(solution)/shard_map/reshape;reshape;reshape | solution.py:42
  21.1 16.8 %shard_map.144 = s32[8,8,128]{2,1,0:T(8,128)S(1)} custom-call(s32[8,128]{1,0:T(8,128)S(1)} %pad.4.refs_0_), custom_call_target="tpu_custom_call" | custom-call | bytes 32768 | tf_op jit(solution)/shard_map/pallas_call | solution.py:99
  38.0 1.3 fusion.7
  39.3 0.2 convert_reduce_fusion
  39.6 0.6 fusion.32
  40.2 0.7 fusion.27
  41.1 0.9 reshape.189
  42.1 3.0 %all-to-all-start.1 = ((bf16[32,100,128]{2,1,0:T(8,128)(2,1)}), bf16[32,100,128]{2,1,0:T(8,128)(2,1)S(1)}, u32[]{:S(2)}, u32[]{:S(2)}) async-start(bf16[32,100,128]{2,1,0:T(8,128)(2,1)} %reshape_reshape_reshape.7), calls=%async_computation.1 | async-start | bytes 1703936 | tf_op jit(solution)/shard_map/all_to_all | solution.py:38
  45.1 12.7 %multiply_convert_fusion = (bf16[320,5120]{1,0:T(8,128)(2,1)S(1)}, f32[320,5120]{1,0:T(8,128)}) fusion(bf16[320,1280]{1,0:T(8,128)(2,1)S(1)} %reshape.189, bf16[1280,5120]{1,0:T(8,128)(2,1)} %param.12), kind=kOutput, calls=%fused_computation.11 | convolution fusion | flops 4209049600 | bytes 23756800 | tf_op jit(solution)/shard_map/dot_general | solution.py:169
  57.7 1.7 %copy-done.9 = bf16[320,5120]{1,0:T(8,128)(2,1)} copy-done((bf16[320,5120]{1,0:T(8,128)(2,1)}, bf16[320,5120]{1,0:T(8,128)(2,1)S(1)}, u32[]{:S(2)}) %copy-start.9) | copy-done | bytes 3276824
  59.4 7.5 %convolution_convert_fusion.4 = bf16[320,1280]{1,0:T(8,128)(2,1)S(1)} fusion(bf16[320,5120]{1,0:T(8,128)(2,1)S(1)} %get-tuple-element.30, bf16[5120,1280]{1,0:T(8,128)(2,1)} %param.13), kind=kOutput, calls=%fused_computation.16 | convolution fusion | flops 4194713600 | bytes 17203200 | tf_op jit(solution)/shard_map/dot_general | solution.py:172
  67.0 1.9 %reshape.190 = bf16[32,100,128]{2,1,0:T(8,128)(2,1)} reshape(bf16[320,1280]{1,0:T(8,128)(2,1)S(1)} %convolution_convert_fusion.4) | data formatting | bytes 1638400 | tf_op jit(solution)/shard_map/reshape | solution.py:42
  68.8 5.9 %all-to-all-start.2 = ((bf16[32,100,128]{2,1,0:T(8,128)(2,1)}), bf16[32,100,128]{2,1,0:T(8,128)(2,1)S(1)}, u32[]{:S(2)}, u32[]{:S(2)}) async-start(bf16[32,100,128]{2,1,0:T(8,128)(2,1)} %reshape.190), calls=%async_computation.2 | async-start | bytes 1703936 | tf_op jit(solution)/shard_map/all_to_all | solution.py:38
  74.7 0.9 reshape.191
  75.7 11.6 %fusion.6 = bf16[320,5120]{1,0:T(8,128)(2,1)S(1)} fusion(f32[320,5120]{1,0:T(8,128)} %get-tuple-element.52, bf16[320,1280]{1,0:T(8,128)(2,1)S(1)} %reshape.191, bf16[5120,1280]{1,0:T(8,128)(2,1)} %param.13), kind=kOutput, calls=%fused_computation.10 | convolution fusion | flops 4227072000 | bytes 23756800 | tf_op jit(solution)/shard_map/dot_general | solution.py:50
  87.3 1.7 %copy-done.8 = bf16[320,5120]{1,0:T(8,128)(2,1)} copy-done((bf16[320,5120]{1,0:T(8,128)(2,1)}, bf16[320,5120]{1,0:T(8,128)(2,1)S(1)}, u32[]{:S(2)}) %copy-start.8) | copy-done | bytes 3276824
  89.0 7.6 %convolution_convert_fusion.3 = bf16[320,1280]{1,0:T(8,128)(2,1)S(1)} fusion(bf16[320,5120]{1,0:T(8,128)(2,1)S(1)} %fusion.6, bf16[1280,5120]{1,0:T(8,128)(2,1)} %param.12), kind=kOutput, calls=%fused_computation.15 | convolution fusion | flops 4194713600 | bytes 17203200 | tf_op jit(solution)/shard_map/dot_general | solution.py:50
  96.6 1.9 %reshape.192 = bf16[32,100,128]{2,1,0:T(8,128)(2,1)} reshape(bf16[320,1280]{1,0:T(8,128)(2,1)S(1)} %convolution_convert_fusion.3) | data formatting | bytes 1638400 | tf_op jit(solution)/shard_map/reshape | solution.py:42
  98.4 12.1 %convolution_convert_fusion.1 = bf16[1280,5120]{1,0:T(8,128)(2,1)} fusion(bf16[320,1280]{1,0:T(8,128)(2,1)S(1)} %reshape.189, bf16[320,5120]{1,0:T(8,128)(2,1)} %copy-done.8), kind=kOutput, calls=%fused_computation.1 | convolution fusion | flops 4200857600 | bytes 17203200 | tf_op jit(solution)/shard_map/dot_general | solution.py:54
  110.6 10.3 %convolution_convert_fusion = bf16[5120,1280]{1,0:T(8,128)(2,1)} fusion(bf16[320,5120]{1,0:T(8,128)(2,1)S(1)} %copy-done.10, bf16[320,1280]{1,0:T(8,128)(2,1)S(1)} %copy-done.4), kind=kOutput, calls=%fused_computation | convolution fusion | flops 4200857600 | bytes 17203200 | tf_op jit(solution)/shard_map/dot_general | solution.py:54
  120.9 5.7 %all-to-all-start.3 = ((bf16[32,100,128]{2,1,0:T(8,128)(2,1)}), bf16[32,100,128]{2,1,0:T(8,128)(2,1)}, u32[]{:S(2)}, u32[]{:S(2)}) async-start(bf16[32,100,128]{2,1,0:T(8,128)(2,1)} %reshape.192), calls=%async_computation.3 | async-start | bytes 1703936 | tf_op jit(solution)/shard_map/all_to_all | solution.py:38
  126.6 1.8 %reshape.193 = bf16[320,1280,1]{1,0,2:T(8,128)(2,1)} reshape(bf16[32,100,128]{2,1,0:T(8,128)(2,1)S(1)} %all-to-all-done.2) | data formatting | bytes 1638400 | tf_op jit(solution)/shard_map/convert_element_type | solution.py:190
  128.4 2.8 %multiply_reduce_fusion = (f32[128,2]{0,1:T(2,128)}, f32[128,1280]{1,0:T(8,128)S(1)}) fusion(f32[128,1280]{1,0:T(8,128)} %convert_element_type.105, f32[128,2]{0,1:T(2,128)S(1)} %copy-done.7, pred[128,2,320]{0,2,1:T(32,128)(4,1)S(1)} %copy-done.5, bf16[320,1280,1]{1,0,2:T(8,128)(2,1)} %reshape.193), kind=kOutput, calls=%fused_computation.20 | convolution fusion | flops 210861824 | bytes 2213888 | tf_op jit(solution)/shard_map/dot_general | solution.py:54
  131.2 0.9 fusion.8
  132.1 3.8 %shard_map.143 = f32[4,2,1280]{2,1,0:T(2,128)S(1)} custom-call(f32[2,1280]{1,0:T(2,128)S(1)} %pad_maximum_fusion.1.refs_0_), custom_call_target="tpu_custom_call" | custom-call | bytes 40960 | tf_op jit(solution)/shard_map/pallas_call | solution.py:99
  136.1 0.2 multiply_reduce_fusion.4
  136.4 6.1 %multiply_reduce_fusion.2 = (f32[2]{0:T(128)S(1)}, bf16[2,4352]{1,0:T(2,128)(2,1)S(1)}) fusion(pred[2,4352]{1,0:T(4,128)(4,1)S(1)} %compare_reduce_fusion, f32[4352]{0:T(1024)S(1)} %fusion.27, bf16[2,1280]{1,0:T(2,128)(2,1)S(1)} %multiply_convert_fusion.3, bf16[1280,4352]{1,0:T(8,128)(2,1)} %param.15), kind=kOutput, calls=%fused_computation.53 | convolution fusion | flops 22700030 | bytes 11189768 | tf_op jit(solution)/shard_map/dot_general | solution.py:213
  142.6 0.5 slice-done.2
  143.1 3.0 %fusion.33 = f32[2,1280]{1,0:T(2,128)S(1)} fusion(bf16[2,4352]{1,0:T(2,128)(2,1)S(1)} %get-tuple-element.50, bf16[1280,4352]{1,0:T(8,128)(2,1)S(1)} %bitcast.43), kind=kOutput, calls=%fused_computation.100 | convolution fusion | flops 22282240 | bytes 11168768 | tf_op jit(solution)/shard_map/dot_general | solution.py:50
  146.2 12.3 %shard_map.145 = (f32[8,2,5632]{2,1,0:T(2,128)S(1)}, f32[4,2,1408]{2,1,0:T(2,128)S(1)}) custom-call(f32[2,5632]{1,0:T(2,128)S(1)} %maximum_convert_fusion.refs_0_, f32[2,1408]{1,0:T(2,128)S(1)} %pad_maximum_fusion.refs_1_), custom_call_target="tpu_custom_call" | custom-call | bytes 405504 | tf_op jit(solution)/shard_map/pallas_call | solution.py:99
  158.5 0.6 slice_reduce_fusion.1
  159.3 2.1 %reshape.194 = bf16[320,1280,1]{1,0,2:T(8,128)(2,1)S(1)} reshape(bf16[32,100,128]{2,1,0:T(8,128)(2,1)} %all-to-all-done.3) | data formatting | bytes 1638400 | tf_op jit(solution)/shard_map/convert_element_type | solution.py:190
  161.4 0.6 convolution_reduce_fusion
  162.0 0.8 add_convert_fusion
  162.8 0.2 multiply_reduce_fusion.5
  163.0 0.7 add_add_fusion
  163.9 1.7 %convolution_convert_fusion.2 = bf16[160,4352]{1,0:T(8,128)(2,1)} fusion(bf16[16,5632]{1,0:T(8,128)(2,1)S(1)} %convert_element_type.125, bf16[16,1280]{1,0:T(8,128)(2,1)S(1)} %slice.31, s32[]{:T(128)S(6)} %select_n.38), kind=kOutput, calls=%fused_computation.12 | convolution fusion | flops 22978560 | bytes 1540100 | tf_op jit(solution)/shard_map/dot_general | solution.py:54
  (69 shorter events, 2.5 us)
Async XLA Ops:
  0.6 16.6 %copy-start = (bf16[128,1280]{1,0:T(8,128)(2,1)S(1)}, bf16[128,1280]{1,0:T(8,128)(2,1)}, u32[]{:S(2)}) copy-start(bf16[128,1280]{1,0:T(8,128)(2,1)} %param.14) | copy-start | bytes 983044
  0.6 16.6 %copy-start.6 = (s32[2,4]{1,0:T(2,128)S(1)}, s32[2,4]{1,0:T(2,128)}, u32[]{:S(2)}) copy-start(s32[2,4]{1,0:T(2,128)} %param.16) | copy-start | bytes 100
  0.7 17.8 %copy-start.7 = (f32[128,2]{0,1:T(2,128)S(1)}, f32[128,2]{0,1:T(2,128)}, u32[]{:S(2)}) copy-start(f32[128,2]{0,1:T(2,128)} %param.11) | copy-start | bytes 3076
  6.9 34.2 %all-to-all-start = ((bf16[32,100,128]{2,1,0:T(8,128)(2,1)}), bf16[32,100,128]{2,1,0:T(8,128)(2,1)S(1)}, u32[]{:S(2)}, u32[]{:S(2)}) async-start(bf16[32,100,128]{2,1,0:T(8,128)(2,1)} %reshape_reshape_reshape.6), calls=%async_computation | async-start | bytes 1703936 | tf_op jit(solution)/shard_map/all_to_all | solution.py:38
  42.1 26.8 %all-to-all-start.1 = ((bf16[32,100,128]{2,1,0:T(8,128)(2,1)}), bf16[32,100,128]{2,1,0:T(8,128)(2,1)S(1)}, u32[]{:S(2)}, u32[]{:S(2)}) async-start(bf16[32,100,128]{2,1,0:T(8,128)(2,1)} %reshape_reshape_reshape.7), calls=%async_computation.1 | async-start | bytes 1703936 | tf_op jit(solution)/shard_map/all_to_all | solution.py:38
  57.7 1.7 %copy-start.9 = (bf16[320,5120]{1,0:T(8,128)(2,1)}, bf16[320,5120]{1,0:T(8,128)(2,1)S(1)}, u32[]{:S(2)}) copy-start(bf16[320,5120]{1,0:T(8,128)(2,1)S(1)} %get-tuple-element.30) | copy-start | bytes 9830404
  68.8 52.1 %all-to-all-start.2 = ((bf16[32,100,128]{2,1,0:T(8,128)(2,1)}), bf16[32,100,128]{2,1,0:T(8,128)(2,1)S(1)}, u32[]{:S(2)}, u32[]{:S(2)}) async-start(bf16[32,100,128]{2,1,0:T(8,128)(2,1)} %reshape.190), calls=%async_computation.2 | async-start | bytes 1703936 | tf_op jit(solution)/shard_map/all_to_all | solution.py:38
  75.6 11.6 %copy-start.3 = (bf16[320,1280]{1,0:T(8,128)(2,1)}, bf16[320,1280]{1,0:T(8,128)(2,1)S(1)}, u32[]{:S(2)}) copy-start(bf16[320,1280]{1,0:T(8,128)(2,1)S(1)} %reshape.191) | copy-start | bytes 2457604
  87.3 1.7 %copy-start.8 = (bf16[320,5120]{1,0:T(8,128)(2,1)}, bf16[320,5120]{1,0:T(8,128)(2,1)S(1)}, u32[]{:S(2)}) copy-start(bf16[320,5120]{1,0:T(8,128)(2,1)S(1)} %fusion.6) | copy-start | bytes 9830404
  98.4 12.1 %copy-start.4 = (bf16[320,1280]{1,0:T(8,128)(2,1)S(1)}, bf16[320,1280]{1,0:T(8,128)(2,1)}, u32[]{:S(2)}) copy-start(bf16[320,1280]{1,0:T(8,128)(2,1)} %copy-done.3) | copy-start | bytes 2457604
  98.4 12.1 %copy-start.10 = (bf16[320,5120]{1,0:T(8,128)(2,1)S(1)}, bf16[320,5120]{1,0:T(8,128)(2,1)}, u32[]{:S(2)}) copy-start(bf16[320,5120]{1,0:T(8,128)(2,1)} %copy-done.9) | copy-start | bytes 9830404
  110.6 17.9 %copy-start.5 = (pred[128,2,320]{0,2,1:T(32,128)(4,1)S(1)}, pred[128,2,320]{0,2,1:T(32,128)(4,1)}, u32[]{:S(2)}) copy-start(pred[128,2,320]{0,2,1:T(32,128)(4,1)} %copy.43) | copy-start | bytes 245764
  110.6 20.6 %copy-start.2 = (bf16[128,1280]{1,0:T(8,128)(2,1)S(1)}, bf16[128,1280]{1,0:T(8,128)(2,1)}, u32[]{:S(2)}) copy-start(bf16[128,1280]{1,0:T(8,128)(2,1)} %param.9) | copy-start | bytes 983044
  120.9 38.4 %all-to-all-start.3 = ((bf16[32,100,128]{2,1,0:T(8,128)(2,1)}), bf16[32,100,128]{2,1,0:T(8,128)(2,1)}, u32[]{:S(2)}, u32[]{:S(2)}) async-start(bf16[32,100,128]{2,1,0:T(8,128)(2,1)} %reshape.192), calls=%async_computation.3 | async-start | bytes 1703936 | tf_op jit(solution)/shard_map/all_to_all | solution.py:38
  128.4 14.1 %slice-start = ((s8[11141120]{0:T(1024)(128)(4,1)}), s8[2752512]{0:T(1024)(128)(4,1)S(1)}, s32[]{:S(2)}) async-start(s8[11141120]{0:T(1024)(128)(4,1)} %bitcast.42), calls=%async_computation.4 | async-start | bytes 5505024
  136.4 6.2 %slice-start.1 = ((s8[11141120]{0:T(1024)(128)(4,1)}), s8[4194304]{0:T(1024)(128)(4,1)S(1)}, s32[]{:S(2)}) async-start(s8[11141120]{0:T(1024)(128)(4,1)} %bitcast.42), calls=%async_computation.5 | async-start | bytes 8388608
  136.4 6.6 %slice-start.2 = ((s8[11141120]{0:T(1024)(128)(4,1)}), s8[4194304]{0:T(1024)(128)(4,1)S(1)}, s32[]{:S(2)}) async-start(s8[11141120]{0:T(1024)(128)(4,1)} %bitcast.42), calls=%async_computation.6 | async-start | bytes 8388608
  143.1 18.9 %copy-start.1 = (bf16[128,1280]{1,0:T(8,128)(2,1)S(1)}, bf16[128,1280]{1,0:T(8,128)(2,1)}, u32[]{:S(2)}) copy-start(bf16[128,1280]{1,0:T(8,128)(2,1)} %param.14) | copy-start | bytes 983044
